TPU v7x, 256 devices: a whole 4x4x8 slice. The times are simulated.
256 devices in a mesh: group: 8 (over x, core), sub: 32 (over y, z).
Axes of the slice: x: 4, y: 4, z: 8, core: 2. Of those that a mesh axis runs over, the one named last changes fastest.
Arguments:
- resid_iface: float32 [256, 16, 4352], P(('group', 'sub')), may hold values from -6 to 6
- resid_inner: float32 [256, 16, 3072], P(('group', 'sub')), may hold values from -6 to 6
- weights: float32 [256, 4352], P(('group', 'sub')), may hold values from 0.25 to 0.75
- nbr: int32 [256, 32], P(('group', 'sub')), may hold values from 0 to 1, as said below
- own2: int32 [256, 128], P(('group', 'sub')), may hold values from 0 to 2047
- cidx: int32 [256, 8], P(('group', 'sub')), may hold values from 0 to 16
- neumann: bfloat16 [256, 17, 256, 256], P(('group', 'sub'))
- dirichlet: bfloat16 [256, 8, 384, 384], P(('group', 'sub'))
- coupling: bfloat16 [256, 8, 256, 384], P(('group', 'sub')), may hold values from -0.375 to 0.375
- coarse_basis: bfloat16 [256, 4352, 128], P(('group', 'sub')), may hold values from -0.5 to 0.5
- group_basis: float32 [16384, 512], P(('group', 'sub')), may hold values from -0.25 to 0.25
- group_inverse: float32 [16384, 2048], P('group', 'sub'), as said below
- top_inverse: float32 [512, 512], replicated, as said below
Outputs:
- interface_out: float32 [256, 16, 4352], P(('group', 'sub'))
- interior_out: float32 [256, 16, 3072], P(('group', 'sub'))
Inputs may be any that keep to these rules, and one draw needn't show every extreme that they name: Symmetric within each group (nbr[(g, q), j] = nbr[(g, j), q]) with nbr[(g, q), q] = 0. `group_inverse`: each matrix of a group is symmetric. `top_inverse`: symmetric.
All inputs are finite; a program needn't handle non-finite values.
Results may differ from a plain program's by a relative error of at most 0.013.
Values may be sent and summed in bfloat16 or wider, within the bound.
A program may use at most 64 MiB of HBM per device.

v0:
```python
import jax
import jax.numpy as jnp
from jax import lax
from jax.sharding import PartitionSpec as P


def padded_2(cells, sides, width):
    for axis, dim in sides:
        count = lax.axis_size(axis)
        ends = count - 1
        head = lax.slice_in_dim(cells, 0, width, axis=dim)
        tail = lax.slice_in_dim(cells, cells.shape[dim] - width, cells.shape[dim], axis=dim)
        cells = jnp.concatenate(
            [
                lax.ppermute(tail, axis, [(i, (i + 1) % count) for i in range(ends)]),
                cells,
                lax.ppermute(head, axis, [((i + 1) % count, i) for i in range(ends)]),
            ],
            axis=dim,
        )
    return cells


def shards(
    resid_iface,
    resid_inner,
    weights,
    nbr,
    own2,
    cidx,
    neumann,
    dirichlet,
    coupling,
    coarse_basis,
    group_basis,
    group_inverse,
    top_inverse,
):
    highest = lax.Precision.HIGHEST
    nsub = lax.axis_size("sub")
    mine = lax.axis_index("sub")
    rows = resid_iface.shape[1]
    width = resid_iface.shape[2]
    slot_width = width // (nsub + 2)
    block_count = neumann.shape[1]
    block_width = neumann.shape[2]
    inner_count = dirichlet.shape[1]
    inner_width = dirichlet.shape[2]
    group_width = group_inverse.shape[0]
    share = group_inverse.shape[1]
    slot_mask = jnp.concatenate([nbr[0].astype(jnp.float32), jnp.ones((2,), jnp.float32)])
    scale = jnp.repeat(slot_mask, slot_width) * weights[0]
    weighted = (scale[None, :] * resid_iface[0]).astype(jnp.bfloat16)
    local0 = jnp.dot(weighted, coarse_basis[0], preferred_element_type=jnp.float32)
    onehot = (own2[0][:, None] == jnp.arange(group_width, dtype=jnp.int32)[None, :]).astype(
        jnp.float32
    )
    contrib = jnp.dot(local0, onehot, precision=highest)
    level2 = lax.psum(contrib.astype(jnp.bfloat16), "sub").astype(jnp.float32)
    level2_mine = lax.dynamic_slice_in_dim(level2, mine * share, share, 1)
    neumann_part = jnp.einsum(
        "rkb,kbc->rkc",
        weighted.reshape(rows, block_count, block_width),
        neumann[0],
        preferred_element_type=jnp.float32,
    ).reshape(rows, width)
    top_term = jnp.dot(level2_mine, group_basis, precision=highest)
    level3 = lax.psum(top_term, ("group", "sub"))
    coarse3 = jnp.dot(level3, top_inverse, precision=highest)
    lifted = lax.dot_general(coarse3, group_basis, (((1,), (1,)), ((), ())), precision=highest)
    coarse2_mine = jnp.dot(level2, group_inverse, precision=highest) + lifted
    coarse2 = lax.all_gather(coarse2_mine.astype(jnp.bfloat16), "sub", axis=1, tiled=True)
    values = jnp.take(coarse2, own2[0], axis=1)
    spread = lax.dot_general(
        values, coarse_basis[0], (((1,), (1,)), ((), ())), preferred_element_type=jnp.float32
    )
    scaled = scale[None, :] * (neumann_part + spread)
    slots = scaled.reshape(rows, nsub + 2, slot_width)
    received = lax.all_to_all(
        slots[:, :nsub, :].astype(jnp.bfloat16), "sub", split_axis=1, concat_axis=1, tiled=True
    ).astype(jnp.float32)
    padded = padded_2(slots[:, nsub:, :], (("group", 1),), 1)
    lower_face = slots[:, nsub, :] + padded[:, 0, :]
    upper_face = slots[:, nsub + 1, :] + padded[:, 3, :]
    total = jnp.concatenate(
        [slots[:, :nsub, :] + received, lower_face[:, None, :], upper_face[:, None, :]], axis=1
    )
    interface_out = total.reshape(rows, width)
    iface_blocks = interface_out.reshape(rows, block_count, block_width).astype(jnp.bfloat16)
    picked = jnp.take(iface_blocks, cidx[0], axis=1)
    pushed = jnp.einsum("rkb,kbc->rkc", picked, coupling[0], preferred_element_type=jnp.float32)
    inner_rhs = (resid_inner[0].reshape(rows, inner_count, inner_width) - pushed).astype(
        jnp.bfloat16
    )
    interior_out = jnp.einsum(
        "rkb,kbc->rkc", inner_rhs, dirichlet[0], preferred_element_type=jnp.float32
    ).reshape(rows, inner_count * inner_width)
    return (interface_out[None], interior_out[None])


def solution(mesh):
    placed = (
        P(("group", "sub"), None, None),
        P(("group", "sub"), None, None),
        P(("group", "sub"), None),
        P(("group", "sub"), None),
        P(("group", "sub"), None),
        P(("group", "sub"), None),
        P(("group", "sub"), None, None, None),
        P(("group", "sub"), None, None, None),
        P(("group", "sub"), None, None, None),
        P(("group", "sub"), None, None),
        P(("group", "sub"), None),
        P("group", "sub"),
        P(),
    )
    return jax.shard_map(
        shards,
        mesh=mesh,
        in_specs=placed,
        out_specs=(P(("group", "sub"), None, None), P(("group", "sub"), None, None)),
        check_vma=False,
    )
```

profile of v0, /device:TPU:1, one launch (start us, length us, event | category | flops | bytes accessed | tf_op | source)
XLA Modules:
  0.0 318.7 jit_solution(4623421728509135453)
XLA Ops:
  7.2 0.0 copy-start
  7.2 0.0 copy-start.2
  7.2 0.0 copy-start.4
  7.2 0.0 copy-start.5
  7.2 0.0 all-reduce.3.cloned.1.call-start
  7.3 0.8 convert_bitcast_fusion
  8.1 0.1 broadcast_bitcast_fusion
  8.1 0.8 fusion.45
  8.9 1.6 fusion.25
  10.5 1.8 convolution_convert_fusion
  12.3 0.0 all-reduce.3.cloned.1.call-update
  12.4 0.0 copy-done.4
  12.4 0.0 copy-done.2
  12.5 0.0 copy-done.5
  12.6 2.0 fusion.7
  14.6 0.7 copy.43
  15.3 0.0 copy-start.1
  15.3 136.0 %all-reduce.3.cloned.1.call-done = bf16[16,2048]{1,0:T(8,128)(2,1)} async-done(((bf16[16,2048]{1,0:T(8,128)(2,1)}), bf16[16,2048]{1,0:T(8,128)(2,1)}) %all-reduce.3.cloned.1.call-update) | async-done | bytes 65552 | tf_op jit(solution)/shard_map/psum | solution.py:59
  151.3 1.7 fusion.47
  153.0 78.0 %psum.15 = f32[16,512]{1,0:T(8,128)S(1)} all-reduce(f32[16,512]{1,0:T(8,128)} %fusion.47), channel_id=1, replica_groups=mesh['group'=8,'sub'=32] {'group','sub'}, use_global_device_ids=true, to_apply=%region_1.0 | all-reduce | flops 8192 | bytes 65536 | tf_op jit(solution)/shard_map/psum | solution.py:68
  231.1 0.0 copy-start.3
  231.1 1.9 fusion.58
  233.0 1.4 fusion.57
  234.4 0.0 copy-done.3
  234.4 0.2 fusion.28
  234.6 35.0 %all-gather = bf16[32,64,16]{1,2,0:T(8,128)(2,1)} all-gather(bf16[1,64,16]{1,2,0:T(8,128)(2,1)S(1)} %fusion.28), channel_id=1, replica_groups=mesh['group'=8,'sub'=32] {'sub'}, dimensions={0}, use_global_device_ids=true | all-gather | bytes 67584 | tf_op jit(solution)/shard_map/all_gather | solution.py:72
  269.6 1.9 copy.41
  271.5 1.8 gather_fusion
  273.3 0.0 copy-done.1
  273.3 2.2 fusion
  275.5 1.0 reshape.101
  276.5 12.7 %collective-permute-start = (f32[16,1,128]{2,1,0:T(1,128)S(1)}, f32[16,1,128]{2,1,0:T(1,128)S(1)}, u32[]{:S(2)}, u32[]{:S(2)}) collective-permute-start(f32[16,1,128]{2,1,0:T(1,128)S(1)} %get-tuple-element.4), channel_id=1, source_target_pairs={{0,32},{32,64},{64,96},{96,128},{128,160},{160,192},{192,224},{1,3... | collective-permute-start | bytes 24584 | tf_op jit(solution)/shard_map/ppermute | solution.py:15
  289.2 1.9 collective-permute-start.1
  291.2 0.7 copy.36
  291.9 5.6 %all-to-all-start = ((bf16[16,32,128]{2,0,1:T(8,128)(2,1)}), bf16[16,32,128]{2,0,1:T(8,128)(2,1)S(1)}, u32[]{:S(2)}, u32[]{:S(2)}) async-start(bf16[16,32,128]{2,0,1:T(8,128)(2,1)} %copy.36), calls=%async_computation | async-start | bytes 262144 | tf_op jit(solution)/shard_map/all_to_all | solution.py:79
  297.5 1.0 copy.45
  298.5 0.0 collective-permute-done
  298.5 0.0 collective-permute-done.1
  298.6 8.8 %all-to-all-done = bf16[16,32,128]{2,0,1:T(8,128)(2,1)S(1)} async-done(((bf16[16,32,128]{2,0,1:T(8,128)(2,1)}), bf16[16,32,128]{2,0,1:T(8,128)(2,1)S(1)}, u32[]{:S(2)}, u32[]{:S(2)}) %all-to-all-start) | async-done | bytes 131104 | tf_op jit(solution)/shard_map/all_to_all | solution.py:79
  307.5 0.1 convert_element_type.48
  307.6 0.6 gather_fusion.1
  308.2 0.0 copy-done
  308.2 2.1 fusion.10
  310.3 0.1 copy.40
  310.4 0.7 broadcast_in_dim_reshape.7
  311.1 0.8 broadcast_in_dim_reshape.6
  (17 shorter events, 0.3 us)
Async XLA Ops:
  7.2 301.0 %copy-start = (bf16[1,8,384,384]{3,2,1,0:T(8,128)(2,1)S(1)}, bf16[1,8,384,384]{3,2,1,0:T(8,128)(2,1)}, u32[]{:S(2)}) copy-start(bf16[1,8,384,384]{3,2,1,0:T(8,128)(2,1)} %param.20) | copy-start | bytes 7077892
  7.2 5.2 %copy-start.2 = (f32[1,16,4352]{2,1,0:T(8,128)S(1)}, f32[1,16,4352]{2,1,0:T(8,128)}, u32[]{:S(2)}) copy-start(f32[1,16,4352]{2,1,0:T(8,128)} %param.13) | copy-start | bytes 835588
  7.2 5.2 %copy-start.4 = (s32[1,128]{1,0:T(1,128)S(1)}, s32[1,128]{1,0:T(1,128)}, u32[]{:S(2)}) copy-start(s32[1,128]{1,0:T(1,128)} %param.17) | copy-start | bytes 1540
  7.2 5.3 %copy-start.5 = (s32[1,8]{1,0:T(1,128)S(1)}, s32[1,8]{1,0:T(1,128)}, u32[]{:S(2)}) copy-start(s32[1,8]{1,0:T(1,128)} %param.18) | copy-start | bytes 100
  7.2 144.1 %all-reduce.3.cloned.1.call-start = ((), (), s32[]{:S(2)}) async-start(), calls=%async_computation.1 | async-start | bytes 131072 | tf_op jit(solution)/shard_map/psum | solution.py:59
  15.3 257.9 %copy-start.1 = (bf16[1,4352,128]{2,1,0:T(8,128)(2,1)S(1)}, bf16[1,4352,128]{2,1,0:T(8,128)(2,1)}, u32[]{:S(2)}) copy-start(bf16[1,4352,128]{2,1,0:T(8,128)(2,1)} %param.22) | copy-start | bytes 3342340
  231.1 3.3 %copy-start.3 = (f32[64,512]{1,0:T(8,128)S(1)}, f32[64,512]{1,0:T(8,128)}, u32[]{:S(2)}) copy-start(f32[64,512]{1,0:T(8,128)} %param.23) | copy-start | bytes 393220
  276.5 22.0 %collective-permute-start = (f32[16,1,128]{2,1,0:T(1,128)S(1)}, f32[16,1,128]{2,1,0:T(1,128)S(1)}, u32[]{:S(2)}, u32[]{:S(2)}) collective-permute-start(f32[16,1,128]{2,1,0:T(1,128)S(1)} %get-tuple-element.4), channel_id=1, source_target_pairs={{0,32},{32,64},{64,96},{96,128},{128,160},{160,192},{192,224},{1,3... | collective-permute-start | bytes 24584 | tf_op jit(solution)/shard_map/ppermute | solution.py:15
  289.2 9.3 %collective-permute-start.1 = (f32[16,1,128]{2,1,0:T(1,128)S(1)}, f32[16,1,128]{2,1,0:T(1,128)S(1)}, u32[]{:S(2)}, u32[]{:S(2)}) collective-permute-start(f32[16,1,128]{2,1,0:T(1,128)S(1)} %get-tuple-element.5), channel_id=1, source_target_pairs={{32,0},{64,32},{96,64},{128,96},{160,128},{192,160},{224,192},{33,... | collective-permute-start | bytes 24584 | tf_op jit(solution)/shard_map/ppermute | solution.py:17
  291.9 15.5 %all-to-all-start = ((bf16[16,32,128]{2,0,1:T(8,128)(2,1)}), bf16[16,32,128]{2,0,1:T(8,128)(2,1)S(1)}, u32[]{:S(2)}, u32[]{:S(2)}) async-start(bf16[16,32,128]{2,0,1:T(8,128)(2,1)} %copy.36), calls=%async_computation | async-start | bytes 262144 | tf_op jit(solution)/shard_map/all_to_all | solution.py:79
Sparse Core Ops, SparseCore 0:
  12.5 138.7 all-reduce.2
where the time goes:
time: 319 us
  waiting for transfers between devices  145 us (45%)
  blocking collectives  113 us (35%)
  starting transfers between devices  20.3 us (6%)
  matrix products  15 us (5%)
  between operations  14.3 us (4%)
  local copies, waits for them, and re-layouts  9.48 us (3%)
    psum x1, waiting for transfers between devices, shards(): level2 = lax.psum(contrib.astype(jnp.bfloat16), 'sub').astype(jnp.float32)  136 us
    psum x1, blocking collectives, shards(): level3 = lax.psum(top_term, ('group', 'sub'))  78 us
    all_gather x1, blocking collectives, shards(): lax.all_gather(coarse2_mine.astype(jnp.bfloat16), 'sub', axis=1, tiled=True)  35 us
    ppermute x1, starting transfers between devices, padded_2(): lax.ppermute(tail, axis, [(i, (i + 1) % count) for i in range(ends)])  12.7 us
    all_to_all x1, waiting for transfers between devices, shards(): lax.all_to_all(slots[:, :nsub, :].astype(jnp.bfloat16), 'sub', split_axis...  8.85 us
  transfers between devices with their start and end apart: 4, of which 2 were waited for; matrix products, arithmetic and copies ran while one was open for 1% of the time, Pallas kernels for 0%

commit v1 on v0

--- a/solution.py
+++ b/solution.py
@@ -65,7 +65,9 @@
         preferred_element_type=jnp.float32,
     ).reshape(rows, width)
     top_term = jnp.dot(level2_mine, group_basis, precision=highest)
-    level3 = lax.psum(top_term, ("group", "sub"))
+    level3 = top_term
+    for mesh_axis in ("group", "sub"):
+        level3 = lax.psum(level3, mesh_axis)
     coarse3 = jnp.dot(level3, top_inverse, precision=highest)
     lifted = lax.dot_general(coarse3, group_basis, (((1,), (1,)), ((), ())), precision=highest)
     coarse2_mine = jnp.dot(level2, group_inverse, precision=highest) + lifted

time: 319 us -> 407 us (1.28)
  blocking collectives: 113 us -> 172 us
  starting transfers between devices: 20.3 us -> 49.7 us
    psum x1 -> x2, blocking collectives: 78 us -> 139 us  [shards(): level3 = lax.psum(level3, mesh_axis)]
    ppermute x1, starting transfers between devices: 12.7 us -> 41 us  [padded_2(): lax.ppermute(tail, axis, [(i, (i + 1) % count) for i in range(ends)])]
where the time goes in v1:
time: 407 us; the launch traced here: 406 us
  blocking collectives  172 us (42%)
  waiting for transfers between devices  145 us (36%)
  starting transfers between devices  49.7 us (12%)
  matrix products  14.4 us (4%)
  between operations  14.3 us (4%)
  local copies, waits for them, and re-layouts  9.48 us (2%)
    psum x2, blocking collectives, shards(): level3 = lax.psum(level3, mesh_axis)  139 us
    psum x1, waiting for transfers between devices, shards(): level2 = lax.psum(contrib.astype(jnp.bfloat16), 'sub').astype(jnp.float32)  136 us
    ppermute x1, starting transfers between devices, padded_2(): lax.ppermute(tail, axis, [(i, (i + 1) % count) for i in range(ends)])  41 us
    all_gather x1, blocking collectives, shards(): lax.all_gather(coarse2_mine.astype(jnp.bfloat16), 'sub', axis=1, tiled=True)  33.2 us
    all_to_all x1, waiting for transfers between devices, shards(): lax.all_to_all(slots[:, :nsub, :].astype(jnp.bfloat16), 'sub', split_axis...  8.92 us
  transfers between devices with their start and end apart: 4, of which 2 were waited for; matrix products, arithmetic and copies ran while one was open for 1% of the time, Pallas kernels for 0%

profile of v1, /device:TPU:1, one launch (start us, length us, event | category | flops | bytes accessed | tf_op | source)
XLA Modules:
  0.0 406.4 jit_solution(16909981359770521150)
XLA Ops:
  7.2 0.0 copy-start
  7.2 0.0 copy-start.2
  7.2 0.0 copy-start.4
  7.2 0.0 copy-start.5
  7.2 0.0 all-reduce.3.cloned.1.call-start
  7.3 0.8 convert_bitcast_fusion
  8.1 0.1 broadcast_bitcast_fusion
  8.1 0.8 fusion.45
  8.9 1.6 fusion.25
  10.5 1.8 convolution_convert_fusion
  12.3 0.0 all-reduce.3.cloned.1.call-update
  12.4 0.0 copy-done.4
  12.4 0.0 copy-done.2
  12.5 0.0 copy-done.5
  12.6 2.0 fusion.7
  14.6 0.7 copy.43
  15.3 0.0 copy-start.1
  15.3 136.0 %all-reduce.3.cloned.1.call-done = bf16[16,2048]{1,0:T(8,128)(2,1)} async-done(((bf16[16,2048]{1,0:T(8,128)(2,1)}), bf16[16,2048]{1,0:T(8,128)(2,1)}) %all-reduce.3.cloned.1.call-update) | async-done | bytes 65552 | tf_op jit(solution)/shard_map/psum | solution.py:59
  151.3 1.1 fusion.47
  152.4 25.3 %psum.22 = f32[16,512]{1,0:T(8,128)} all-reduce(f32[16,512]{1,0:T(8,128)S(1)} %fusion.47), channel_id=1, replica_groups=mesh['group'=8,'sub'=32] {'group'}, use_global_device_ids=true, to_apply=%region_1.0 | all-reduce | flops 8192 | bytes 65536 | tf_op jit(solution)/shard_map/psum | solution.py:70
  177.8 113.4 %psum.23 = f32[16,512]{1,0:T(8,128)S(1)} all-reduce(f32[16,512]{1,0:T(8,128)} %psum.22), channel_id=1, replica_groups=mesh['group'=8,'sub'=32] {'sub'}, use_global_device_ids=true, to_apply=%region_2.0 | all-reduce | flops 8192 | bytes 65536 | tf_op jit(solution)/shard_map/psum | solution.py:70
  291.1 0.0 copy-start.3
  291.1 1.9 fusion.58
  293.0 1.4 fusion.57
  294.4 0.0 copy-done.3
  294.4 0.2 fusion.28
  294.7 33.2 %all-gather = bf16[32,64,16]{1,2,0:T(8,128)(2,1)} all-gather(bf16[1,64,16]{1,2,0:T(8,128)(2,1)S(1)} %fusion.28), channel_id=1, replica_groups=mesh['group'=8,'sub'=32] {'sub'}, dimensions={0}, use_global_device_ids=true | all-gather | bytes 67584 | tf_op jit(solution)/shard_map/all_gather | solution.py:74
  327.9 1.9 copy.41
  329.8 1.8 gather_fusion
  331.5 0.0 copy-done.1
  331.5 2.2 fusion
  333.7 1.0 reshape.101
  334.8 41.0 %collective-permute-start = (f32[16,1,128]{2,1,0:T(1,128)S(1)}, f32[16,1,128]{2,1,0:T(1,128)S(1)}, u32[]{:S(2)}, u32[]{:S(2)}) collective-permute-start(f32[16,1,128]{2,1,0:T(1,128)S(1)} %get-tuple-element.4), channel_id=1, source_target_pairs={{0,32},{32,64},{64,96},{96,128},{128,160},{160,192},{192,224},{1,3... | collective-permute-start | bytes 24584 | tf_op jit(solution)/shard_map/ppermute | solution.py:15
  375.8 3.1 collective-permute-start.1
  378.9 0.7 copy.36
  379.6 5.5 %all-to-all-start = ((bf16[16,32,128]{2,0,1:T(8,128)(2,1)}), bf16[16,32,128]{2,0,1:T(8,128)(2,1)S(1)}, u32[]{:S(2)}, u32[]{:S(2)}) async-start(bf16[16,32,128]{2,0,1:T(8,128)(2,1)} %copy.36), calls=%async_computation | async-start | bytes 262144 | tf_op jit(solution)/shard_map/all_to_all | solution.py:81
  385.2 1.0 copy.45
  386.2 0.0 collective-permute-done
  386.2 0.0 collective-permute-done.1
  386.2 8.9 %all-to-all-done = bf16[16,32,128]{2,0,1:T(8,128)(2,1)S(1)} async-done(((bf16[16,32,128]{2,0,1:T(8,128)(2,1)}), bf16[16,32,128]{2,0,1:T(8,128)(2,1)S(1)}, u32[]{:S(2)}, u32[]{:S(2)}) %all-to-all-start) | async-done | bytes 131104 | tf_op jit(solution)/shard_map/all_to_all | solution.py:81
  395.3 0.1 convert_element_type.48
  395.4 0.6 gather_fusion.1
  395.9 0.0 copy-done
  395.9 2.1 fusion.10
  398.1 0.1 copy.40
  398.1 0.7 broadcast_in_dim_reshape.7
  398.8 0.8 broadcast_in_dim_reshape.6
  (17 shorter events, 0.3 us)
Async XLA Ops:
  7.2 388.8 %copy-start = (bf16[1,8,384,384]{3,2,1,0:T(8,128)(2,1)S(1)}, bf16[1,8,384,384]{3,2,1,0:T(8,128)(2,1)}, u32[]{:S(2)}) copy-start(bf16[1,8,384,384]{3,2,1,0:T(8,128)(2,1)} %param.20) | copy-start | bytes 7077892
  7.2 5.2 %copy-start.2 = (f32[1,16,4352]{2,1,0:T(8,128)S(1)}, f32[1,16,4352]{2,1,0:T(8,128)}, u32[]{:S(2)}) copy-start(f32[1,16,4352]{2,1,0:T(8,128)} %param.13) | copy-start | bytes 835588
  7.2 5.2 %copy-start.4 = (s32[1,128]{1,0:T(1,128)S(1)}, s32[1,128]{1,0:T(1,128)}, u32[]{:S(2)}) copy-start(s32[1,128]{1,0:T(1,128)} %param.17) | copy-start | bytes 1540
  7.2 5.3 %copy-start.5 = (s32[1,8]{1,0:T(1,128)S(1)}, s32[1,8]{1,0:T(1,128)}, u32[]{:S(2)}) copy-start(s32[1,8]{1,0:T(1,128)} %param.18) | copy-start | bytes 100
  7.2 144.1 %all-reduce.3.cloned.1.call-start = ((), (), s32[]{:S(2)}) async-start(), calls=%async_computation.1 | async-start | bytes 131072 | tf_op jit(solution)/shard_map/psum | solution.py:59
  15.3 316.2 %copy-start.1 = (bf16[1,4352,128]{2,1,0:T(8,128)(2,1)S(1)}, bf16[1,4352,128]{2,1,0:T(8,128)(2,1)}, u32[]{:S(2)}) copy-start(bf16[1,4352,128]{2,1,0:T(8,128)(2,1)} %param.22) | copy-start | bytes 3342340
  291.1 3.3 copy-start.3
  334.8 51.4 %collective-permute-start = (f32[16,1,128]{2,1,0:T(1,128)S(1)}, f32[16,1,128]{2,1,0:T(1,128)S(1)}, u32[]{:S(2)}, u32[]{:S(2)}) collective-permute-start(f32[16,1,128]{2,1,0:T(1,128)S(1)} %get-tuple-element.4), channel_id=1, source_target_pairs={{0,32},{32,64},{64,96},{96,128},{128,160},{160,192},{192,224},{1,3... | collective-permute-start | bytes 24584 | tf_op jit(solution)/shard_map/ppermute | solution.py:15
  375.8 10.4 %collective-permute-start.1 = (f32[16,1,128]{2,1,0:T(1,128)S(1)}, f32[16,1,128]{2,1,0:T(1,128)S(1)}, u32[]{:S(2)}, u32[]{:S(2)}) collective-permute-start(f32[16,1,128]{2,1,0:T(1,128)S(1)} %get-tuple-element.5), channel_id=1, source_target_pairs={{32,0},{64,32},{96,64},{128,96},{160,128},{192,160},{224,192},{33,... | collective-permute-start | bytes 24584 | tf_op jit(solution)/shard_map/ppermute | solution.py:17
  379.6 15.5 %all-to-all-start = ((bf16[16,32,128]{2,0,1:T(8,128)(2,1)}), bf16[16,32,128]{2,0,1:T(8,128)(2,1)S(1)}, u32[]{:S(2)}, u32[]{:S(2)}) async-start(bf16[16,32,128]{2,0,1:T(8,128)(2,1)} %copy.36), calls=%async_computation | async-start | bytes 262144 | tf_op jit(solution)/shard_map/all_to_all | solution.py:81
Sparse Core Ops, SparseCore 0:
  12.5 138.7 all-reduce.2
